TPU v7x, 512 devices: a whole 4x4x16 slice. The times are simulated.
512 devices in a mesh: head: 32 (over z, core), req: 16 (over y, x).
Axes of the slice: x: 4, y: 4, z: 16, core: 2. Of those that a mesh axis runs over, the one named last changes fastest.
Arguments:
- queries: bfloat16 [65536, 4096], P(('req', 'head')), parts along dimension 0, may hold values from -120 to 120
- keys_new: bfloat16 [65536, 1024], P(('req', 'head')), parts along dimension 0, may hold values from -6 to 6
- values_new: bfloat16 [65536, 1024], P(('req', 'head')), parts along dimension 0, may hold values from -18 to 18
- prefix_keys: bfloat16 [262144, 1024], P(('req', 'head')), parts along dimension 0, may hold values from -6 to 6
- prefix_values: bfloat16 [262144, 1024], P(('req', 'head')), parts along dimension 0, may hold values from -18 to 18
- vertical_blocks: int32 [512, 32], P('req'), parts along dimension 0, may hold values from 0 to 255, as said below
- vertical_counts: int32 [512], P('req'), parts along dimension 0, may hold values from 4 to 32, as said below
- slash_offsets: int32 [512, 8], P('req'), parts along dimension 0, may hold values from 0 to 63, as said below
- slash_counts: int32 [512], P('req'), parts along dimension 0, may hold values from 1 to 8
Outputs:
- attended: bfloat16 [65536, 4096], P(('req', 'head')), parts along dimension 0
There are 16 independent parts, one for each index of `req`. A program takes and returns all parts, laid end to end along the dimension named above; each array names one. Nothing has to cross between parts.
Inputs may be any that keep to these rules, and one draw needn't show every extreme that they name: `vertical_blocks`: the 32 entries of one head's list lie in distinct ranges of 8 blocks (range r holds blocks r * 8 to (r + 1) * 8 - 1), so each range holds at most one; unused entries are valid blocks too; some head lists a block in every range. `vertical_counts`: one head uses all 32 entries. `slash_offsets`: each head's first offset is 0 and its offsets are distinct.
All inputs are finite; a program needn't handle non-finite values.
Results may differ from a plain program's by a relative error of at most 0.0039.
Values may be sent and summed in bfloat16 or wider, within the bound.
A program may use at most 64 MiB of HBM per device.

v0:
```python
import math

import jax
import jax.numpy as jnp
from jax import lax
from jax.sharding import PartitionSpec as P

H = 32
KVH = 8
HD = 128
BLK = 64


def slash_part(q_rows, key_blocks, value_blocks, offsets, slash_total, first_block, score_scale):
    row_blocks = q_rows.shape[0] // BLK
    blocks = first_block + jnp.arange(row_blocks, dtype=jnp.int32)
    target = blocks[:, None] - offsets[None, :]
    usable = (target >= 0) & (jnp.arange(offsets.shape[0], dtype=jnp.int32)[None, :] < slash_total)
    picked = jnp.maximum(target, 0)
    near_keys = key_blocks[picked].reshape(row_blocks, -1, HD)
    near_values = value_blocks[picked].reshape(row_blocks, -1, HD)
    scores = (
        jnp.einsum(
            "prd,pkd->prk",
            q_rows.reshape(row_blocks, BLK, HD),
            near_keys,
            preferred_element_type=jnp.float32,
        )
        * score_scale
    )
    within = jnp.arange(BLK)[None, :] <= jnp.arange(BLK)[:, None]
    allowed = usable[:, None, :, None] & (
        within[None, :, None, :] | (offsets != 0)[None, None, :, None]
    )
    scores = jnp.where(allowed.reshape(row_blocks, BLK, -1), scores, -jnp.inf)
    return (scores, near_values)


def attend(q_head, k_head, v_head, far_keys, far_values, slot_live, offsets, slash_total):
    span_rows = q_head.shape[0]
    slot_count = far_keys.shape[0]
    score_scale = 1.0 / math.sqrt(HD)
    group_rows = math.gcd(span_rows, 512)
    row_blocks = group_rows // BLK
    key_blocks = k_head.reshape(span_rows // BLK, BLK, HD)
    value_blocks = v_head.reshape(span_rows // BLK, BLK, HD)
    flat_keys = far_keys.reshape(slot_count * BLK, HD)
    flat_values = far_values.reshape(slot_count * BLK, HD)
    live_cols = jnp.repeat(slot_live, BLK)

    def group_output(first_block):
        q_rows = lax.dynamic_slice_in_dim(q_head, first_block * BLK, group_rows, 0)
        near_scores, near_values = slash_part(
            q_rows, key_blocks, value_blocks, offsets, slash_total, first_block, score_scale
        )
        near_top = jnp.max(near_scores, 2)
        far_scores = (
            jnp.einsum("rd,kd->rk", q_rows, flat_keys, preferred_element_type=jnp.float32)
            * score_scale
        )
        far_scores = jnp.where(live_cols[None, :], far_scores, -jnp.inf).reshape(
            row_blocks, BLK, -1
        )
        row_top = jnp.maximum(near_top, jnp.max(far_scores, 2))
        far_weights = jnp.exp(far_scores - row_top[..., None])
        near_weights = jnp.exp(near_scores - row_top[..., None])
        row_total = jnp.sum(far_weights, 2) + jnp.sum(near_weights, 2)
        mixed_rows = jnp.dot(
            far_weights.astype(jnp.bfloat16).reshape(group_rows, -1),
            flat_values,
            preferred_element_type=jnp.float32,
        ).reshape(row_blocks, BLK, HD)
        mixed_rows = mixed_rows + jnp.einsum(
            "prk,pkd->prd",
            near_weights.astype(jnp.bfloat16),
            near_values,
            preferred_element_type=jnp.float32,
        )
        return (mixed_rows / row_total[..., None]).reshape(group_rows, HD)

    starts = jnp.arange(span_rows // group_rows, dtype=jnp.int32) * row_blocks
    return lax.map(group_output, starts).reshape(span_rows, HD)


def shards(
    queries,
    keys_new,
    values_new,
    prefix_keys,
    prefix_values,
    vertical_blocks,
    vertical_counts,
    slash_offsets,
    slash_counts,
):
    devices = lax.axis_size("head")
    device_index = lax.axis_index("head")
    tok_rows = queries.shape[0]
    local_heads = H // devices
    group_size = H // KVH

    def repeat_heads(source):
        return jnp.broadcast_to(
            source.reshape(tok_rows, KVH, 1, HD), (tok_rows, KVH, group_size, HD)
        ).reshape(tok_rows, H * HD)

    q_local, k_local, v_local = (
        lax.all_to_all(queries, "head", split_axis=1, concat_axis=0, tiled=True),
        lax.all_to_all(repeat_heads(keys_new), "head", split_axis=1, concat_axis=0, tiled=True),
        lax.all_to_all(repeat_heads(values_new), "head", split_axis=1, concat_axis=0, tiled=True),
    )
    own_blocks = prefix_keys.shape[0] // BLK
    list_length = vertical_blocks.shape[1]
    owner_of = vertical_blocks // own_blocks
    live_entry = jnp.arange(list_length, dtype=jnp.int32)[None, :] < vertical_counts[:, None]
    mine_entry = live_entry & (owner_of == device_index)
    local_block = jnp.sum(jnp.where(mine_entry, vertical_blocks - device_index * own_blocks, 0), 1)
    kv_of_head = jnp.arange(H, dtype=jnp.int32) // group_size
    send_keys = prefix_keys.reshape(own_blocks, BLK, KVH, HD)[local_block, :, kv_of_head, :]
    send_values = prefix_values.reshape(own_blocks, BLK, KVH, HD)[local_block, :, kv_of_head, :]
    got_keys, got_values = (
        lax.all_to_all(send_keys, "head", split_axis=0, concat_axis=0, tiled=True),
        lax.all_to_all(send_values, "head", split_axis=0, concat_axis=0, tiled=True),
    )
    got_keys = got_keys.reshape(devices, local_heads, BLK, HD)
    got_values = got_values.reshape(devices, local_heads, BLK, HD)
    my_owner = lax.dynamic_slice_in_dim(owner_of, device_index * local_heads, local_heads, 0)
    my_live = lax.dynamic_slice_in_dim(live_entry, device_index * local_heads, local_heads, 0)
    slot_live = jnp.any(
        my_live[:, :, None]
        & (my_owner[:, :, None] == jnp.arange(devices, dtype=jnp.int32)[None, None, :]),
        1,
    )
    head_index = device_index * local_heads + 0
    result = attend(
        q_local,
        k_local,
        v_local,
        got_keys[:, 0],
        got_values[:, 0],
        slot_live[0],
        slash_offsets[head_index],
        slash_counts[head_index],
    )
    outputs = result.astype(jnp.bfloat16)
    return lax.all_to_all(outputs, "head", split_axis=0, concat_axis=1, tiled=True)


def solution(mesh):
    return jax.shard_map(
        shards,
        mesh=mesh,
        in_specs=(
            P(("req", "head"), None),
            P(("req", "head"), None),
            P(("req", "head"), None),
            P(("req", "head"), None),
            P(("req", "head"), None),
            P("req", None),
            P("req"),
            P("req", None),
            P("req"),
        ),
        out_specs=P(("req", "head"), None),
        check_vma=False,
    )
```

profile of v0, /device:TPU:1, one launch (start us, length us, event | category | flops | bytes accessed | tf_op | source)
XLA Modules:
  0.0 505.4 jit_solution(9643083838674255750)
XLA Ops:
  0.0 1.6 copy.53
  2.2 1.4 gather_fusion.2
  3.6 16.8 %all-to-all-start.1 = ((bf16[32,64,128]{2,1,0:T(8,128)(2,1)}), bf16[32,64,128]{2,1,0:T(8,128)(2,1)}, u32[]{:S(2)}, u32[]{:S(2)}) async-start(bf16[32,64,128]{2,1,0:T(8,128)(2,1)} %gather_fusion.2), calls=%async_computation.1 | async-start | bytes 1048576 | tf_op jit(solution)/shard_map/all_to_all | solution.py:122
  21.0 1.4 gather_fusion.3
  22.4 31.5 %all-to-all-done.1 = bf16[32,64,128]{2,1,0:T(8,128)(2,1)} async-done(((bf16[32,64,128]{2,1,0:T(8,128)(2,1)}), bf16[32,64,128]{2,1,0:T(8,128)(2,1)}, u32[]{:S(2)}, u32[]{:S(2)}) %all-to-all-start.1) | async-done | bytes 524320 | tf_op jit(solution)/shard_map/all_to_all | solution.py:122
  54.0 4.7 all-to-all-start.3
  58.7 1.3 copy_bitcast_fusion
  60.0 32.3 %all-to-all-done.3 = bf16[32,64,128]{2,1,0:T(8,128)(2,1)} async-done(((bf16[32,64,128]{2,1,0:T(8,128)(2,1)}), bf16[32,64,128]{2,1,0:T(8,128)(2,1)}, u32[]{:S(2)}, u32[]{:S(2)}) %all-to-all-start.3) | async-done | bytes 524320 | tf_op jit(solution)/shard_map/all_to_all | solution.py:123
  92.3 5.1 all-to-all-start
  97.4 55.8 %all-to-all-done = bf16[128,32,128]{2,0,1:T(8,128)(2,1)} async-done(((bf16[128,32,128]{2,0,1:T(8,128)(2,1)}), bf16[128,32,128]{2,0,1:T(8,128)(2,1)}, u32[]{:S(2)}, u32[]{:S(2)}) %all-to-all-start) | async-done | bytes 1048608 | tf_op jit(solution)/shard_map/all_to_all | solution.py:108
  154.4 5.3 %all-to-all-start.2 = ((bf16[128,32,128]{2,0,1:T(8,128)(2,1)}), bf16[128,32,128]{2,0,1:T(8,128)(2,1)}, u32[]{:S(2)}, u32[]{:S(2)}) async-start(bf16[128,32,128]{2,0,1:T(8,128)(2,1)} %bitcast.7), calls=%async_computation.2 | async-start | bytes 2097152 | tf_op jit(solution)/shard_map/all_to_all | solution.py:109
  159.8 55.8 %all-to-all-done.2 = bf16[128,32,128]{2,0,1:T(8,128)(2,1)} async-done(((bf16[128,32,128]{2,0,1:T(8,128)(2,1)}), bf16[128,32,128]{2,0,1:T(8,128)(2,1)}, u32[]{:S(2)}, u32[]{:S(2)}) %all-to-all-start.2) | async-done | bytes 1048608 | tf_op jit(solution)/shard_map/all_to_all | solution.py:109
  216.8 5.3 %all-to-all-start.4 = ((bf16[128,32,128]{2,0,1:T(8,128)(2,1)}), bf16[128,32,128]{2,0,1:T(8,128)(2,1)}, u32[]{:S(2)}, u32[]{:S(2)}) async-start(bf16[128,32,128]{2,0,1:T(8,128)(2,1)} %bitcast.11), calls=%async_computation.4 | async-start | bytes 2097152 | tf_op jit(solution)/shard_map/all_to_all | solution.py:110
  224.2 53.8 %all-to-all-done.4 = bf16[128,32,128]{2,0,1:T(8,128)(2,1)} async-done(((bf16[128,32,128]{2,0,1:T(8,128)(2,1)}), bf16[128,32,128]{2,0,1:T(8,128)(2,1)}, u32[]{:S(2)}, u32[]{:S(2)}) %all-to-all-start.4) | async-done | bytes 1048608 | tf_op jit(solution)/shard_map/all_to_all | solution.py:110
  278.0 165.0 %while.11 = (s32[]{:T(128)}, bf16[8,512,128]{2,1,0:T(8,128)(2,1)}, s32[8]{0:T(128)}, bf16[4096,128]{1,0:T(8,128)(2,1)}, bf16[2048,128]{1,0:T(8,128)(2,1)}, /*ind...) while((s32[]{:T(128)}, bf16[8,512,128]{2,1,0:T(8,128)(2,1)}, ...), condition=%wide.region_7.8_spmd.clone, body=%wide.region_2.7_spmd.clone.sunk | while | flops 681808704 | bytes 24797288 | solution.py:82
  278.8 1.3 dynamic_slice.40
  281.6 3.7 fusion.58
  286.1 2.0 gather_fusion
  290.1 3.2 fusion.61
  293.3 1.8 fusion.62
  295.0 2.0 gather_fusion.1
  299.4 1.3 dynamic_slice.40
  302.2 3.7 fusion.58
  306.7 2.0 gather_fusion
  310.7 3.2 fusion.61
  313.9 1.7 fusion.62
  315.6 2.0 gather_fusion.1
  320.0 1.3 dynamic_slice.40
  322.8 3.7 fusion.58
  327.3 2.0 gather_fusion
  331.3 3.2 fusion.61
  334.5 1.8 fusion.62
  336.3 2.0 gather_fusion.1
  340.6 1.3 dynamic_slice.40
  343.4 3.7 fusion.58
  348.0 2.0 gather_fusion
  351.9 3.2 fusion.61
  355.1 1.8 fusion.62
  356.9 2.0 gather_fusion.1
  361.3 1.3 dynamic_slice.40
  364.1 3.7 fusion.58
  368.6 2.0 gather_fusion
  372.5 3.2 fusion.61
  375.7 1.8 fusion.62
  377.5 2.0 gather_fusion.1
  381.9 1.3 dynamic_slice.40
  384.7 3.7 fusion.58
  389.2 2.0 gather_fusion
  393.2 3.2 fusion.61
  396.4 1.8 fusion.62
  398.1 2.0 gather_fusion.1
  402.5 1.3 dynamic_slice.40
  405.3 3.7 fusion.58
  409.8 2.0 gather_fusion
  413.8 3.2 fusion.61
  417.0 1.8 fusion.62
  418.7 2.0 gather_fusion.1
  425.9 3.7 fusion.58
  430.4 2.0 gather_fusion
  434.4 3.2 fusion.61
  437.6 1.8 fusion.62
  439.4 2.0 gather_fusion.1
  443.0 60.4 %all_to_all.77 = bf16[32,128,128]{2,1,0:T(8,128)(2,1)S(1)} all-to-all(bf16[32,128,128]{2,1,0:T(8,128)(2,1)} %bitcast.106), channel_id=1, replica_groups=mesh['head'=32,'req'=16] {'head'}, dimensions={0} | all-to-all | bytes 2097152 | tf_op jit(solution)/shard_map/all_to_all | solution.py:146
  504.1 1.3 copy.48
  (252 shorter events, 55.7 us)
Async XLA Ops:
  0.0 58.7 %copy-start = (bf16[128,4096]{1,0:T(8,128)(2,1)S(1)}, bf16[128,4096]{1,0:T(8,128)(2,1)}, u32[]{:S(2)}) copy-start(bf16[128,4096]{1,0:T(8,128)(2,1)} %param.11) | copy-start | bytes 3145732
  0.0 1.9 copy-start.4
  0.0 2.0 copy-start.6
  0.0 20.4 %copy-start.1 = (bf16[512,1024]{1,0:T(8,128)(2,1)S(1)}, bf16[512,1024]{1,0:T(8,128)(2,1)}, u32[]{:S(2)}) copy-start(bf16[512,1024]{1,0:T(8,128)(2,1)} %param.15) | copy-start | bytes 3145732
  3.6 50.4 %all-to-all-start.1 = ((bf16[32,64,128]{2,1,0:T(8,128)(2,1)}), bf16[32,64,128]{2,1,0:T(8,128)(2,1)}, u32[]{:S(2)}, u32[]{:S(2)}) async-start(bf16[32,64,128]{2,1,0:T(8,128)(2,1)} %gather_fusion.2), calls=%async_computation.1 | async-start | bytes 1048576 | tf_op jit(solution)/shard_map/all_to_all | solution.py:122
  20.7 76.6 %copy-start.2 = (bf16[128,1024]{1,0:T(8,128)(2,1)S(1)}, bf16[128,1024]{1,0:T(8,128)(2,1)}, u32[]{:S(2)}) copy-start(bf16[128,1024]{1,0:T(8,128)(2,1)} %param.12) | copy-start | bytes 786436
  54.0 38.3 %all-to-all-start.3 = ((bf16[32,64,128]{2,1,0:T(8,128)(2,1)}), bf16[32,64,128]{2,1,0:T(8,128)(2,1)}, u32[]{:S(2)}, u32[]{:S(2)}) async-start(bf16[32,64,128]{2,1,0:T(8,128)(2,1)} %gather_fusion.3), calls=%async_computation.3 | async-start | bytes 1048576 | tf_op jit(solution)/shard_map/all_to_all | solution.py:123
  58.7 101.0 %copy-start.3 = (bf16[128,1024]{1,0:T(8,128)(2,1)S(1)}, bf16[128,1024]{1,0:T(8,128)(2,1)}, u32[]{:S(2)}) copy-start(bf16[128,1024]{1,0:T(8,128)(2,1)} %param.13) | copy-start | bytes 786436
  92.3 60.9 %all-to-all-start = ((bf16[128,32,128]{2,0,1:T(8,128)(2,1)}), bf16[128,32,128]{2,0,1:T(8,128)(2,1)}, u32[]{:S(2)}, u32[]{:S(2)}) async-start(bf16[128,32,128]{2,0,1:T(8,128)(2,1)} %copy_bitcast_fusion), calls=%async_computation | async-start | bytes 2097152 | tf_op jit(solution)/shard_map/all_to_all | solution.py:108
  97.4 124.8 %copy-start.5 = (s32[32,8]{0,1:T(8,128)S(1)}, s32[32,8]{0,1:T(8,128)}, u32[]{:S(2)}) copy-start(s32[32,8]{0,1:T(8,128)} %param.18) | copy-start | bytes 3076
  97.4 124.9 %copy-start.7 = (s32[32]{0:T(128)S(1)}, s32[32]{0:T(128)}, u32[]{:S(2)}) copy-start(s32[32]{0:T(128)} %param.19) | copy-start | bytes 388
  154.4 61.2 %all-to-all-start.2 = ((bf16[128,32,128]{2,0,1:T(8,128)(2,1)}), bf16[128,32,128]{2,0,1:T(8,128)(2,1)}, u32[]{:S(2)}, u32[]{:S(2)}) async-start(bf16[128,32,128]{2,0,1:T(8,128)(2,1)} %bitcast.7), calls=%async_computation.2 | async-start | bytes 2097152 | tf_op jit(solution)/shard_map/all_to_all | solution.py:109
  216.8 61.2 %all-to-all-start.4 = ((bf16[128,32,128]{2,0,1:T(8,128)(2,1)}), bf16[128,32,128]{2,0,1:T(8,128)(2,1)}, u32[]{:S(2)}, u32[]{:S(2)}) async-start(bf16[128,32,128]{2,0,1:T(8,128)(2,1)} %bitcast.11), calls=%async_computation.4 | async-start | bytes 2097152 | tf_op jit(solution)/shard_map/all_to_all | solution.py:110
where the time goes:
time: 508 us; the launch traced here: 505 us
  waiting for transfers between devices  229 us (45%)
  local copies, waits for them, and re-layouts  79.3 us (16%)
  blocking collectives  60.4 us (12%)
  matrix products  51.3 us (10%)
  other arithmetic  42 us (8%)
  starting transfers between devices  37.1 us (7%)
  loops' own time  5.78 us (1%)
    all_to_all x1, blocking collectives, shards(): lax.all_to_all(outputs, 'head', split_axis=0, concat_axis=1, tiled=True)  60.4 us
    all_to_all x1, waiting for transfers between devices, shards(): lax.all_to_all(repeat_heads(keys_new), 'head', split_axis=1, concat_axis=...  55.8 us
    all_to_all x1, waiting for transfers between devices, shards(): lax.all_to_all(queries, 'head', split_axis=1, concat_axis=0, tiled=True)  55.8 us
    all_to_all x1, waiting for transfers between devices, shards(): lax.all_to_all(repeat_heads(values_new), 'head', split_axis=1, concat_axi...  53.8 us
    all_to_all x1, waiting for transfers between devices, shards(): lax.all_to_all(send_values, 'head', split_axis=0, concat_axis=0, tiled=True)  32.3 us
    all_to_all x1, waiting for transfers between devices, shards(): lax.all_to_all(send_keys, 'head', split_axis=0, concat_axis=0, tiled=True)  31.5 us
    dot_general x8, matrix products, group_output(): jnp.einsum('rd,kd->rk', q_rows, flat_keys, preferred_element_type=jnp.flo...  29.7 us
    reduce_sum x16, other arithmetic, group_output(): row_total = jnp.sum(far_weights, 2) + jnp.sum(near_weights, 2)  28.4 us
  transfers between devices with their start and end apart: 5, of which 5 were waited for; matrix products, arithmetic and copies ran while one was open for 1% of the time, Pallas kernels for 0%

commit v1 on v0

v1 whole, which is shorter than its diff:
```python
import math

import jax
import jax.numpy as jnp
from jax import lax
from jax.experimental import pallas as pl
from jax.experimental.pallas import tpu as pltpu
from jax.sharding import PartitionSpec as P

H = 32
KVH = 8
HD = 128
BLK = 64
SMAX = 8
DEV = 32
CHIPS = 16
OWN = 8
TOK = 128
FAR = DEV * BLK
NEAR = SMAX * BLK
MESH = pl.DeviceIdType.MESH
SCALE = math.log2(math.e) / math.sqrt(HD)
NEG = -math.inf


def kernel(
    q,
    k,
    v,
    pk,
    pv,
    vb,
    vc,
    so,
    sc,
    out,
    kv,
    far,
    far_send,
    pkb,
    pvb,
    qb,
    ob,
    far_bias,
    tri,
    load_sem,
    near_sem,
    near_send_sem,
    far_sem,
    far_send_sem,
    q_sem,
    q_send_sem,
    out_sem,
    out_send_sem,
):
    me = lax.axis_index("head")
    z, c = lax.div(me, 2), lax.rem(me, 2)
    g, odd = lax.div(z, 2), lax.rem(z, 2)
    sibling = 2 * z + 1 - c
    across = 2 * (2 * g + 1 - odd) + c

    def columns(index):
        return pl.ds(pl.multiple_of(index * HD, HD), HD)

    def remote(src, dst, send_sem, recv_sem, device):
        return pltpu.make_async_remote_copy(
            src_ref=src,
            dst_ref=dst,
            send_sem=send_sem,
            recv_sem=recv_sem,
            device_id={"head": device},
            device_id_type=MESH,
        )

    def wait_bytes(ref, sem):
        pltpu.make_async_copy(ref, ref, sem).wait()

    barrier = pltpu.get_barrier_semaphore()

    def greet(j, carry):
        pl.semaphore_signal(
            barrier, inc=1, device_id={"head": lax.rem(me + j, DEV)}, device_id_type=MESH
        )
        return carry

    lax.fori_loop(1, DEV, greet, 0)
    load_k = pltpu.make_async_copy(pk, pkb, load_sem.at[0])
    load_v = pltpu.make_async_copy(pv, pvb, load_sem.at[1])
    load_k.start()
    load_v.start()

    spot = 15 * (1 - odd)
    own_k = pltpu.make_async_copy(k.at[:, :, columns(g)], kv.at[c, spot, 0], load_sem.at[2])
    own_v = pltpu.make_async_copy(v.at[:, :, columns(g)], kv.at[c, spot, 1], load_sem.at[3])
    own_k.start()
    own_v.start()
    pltpu.make_async_copy(q.at[:, columns(me)], qb.at[me], q_sem.at[z]).start()

    pl.semaphore_wait(barrier, DEV - 1)

    def near_out(j, carry):
        group = lax.rem(g + j, KVH)
        chip = 2 * group + lax.div(lax.rem(2 * group - z + CHIPS, CHIPS), CHIPS // 2)
        place = lax.rem(z - 2 * group - 1 + 2 * CHIPS, CHIPS)
        for part, source in enumerate((k, v)):
            remote(
                source.at[:, :, columns(group)],
                kv.at[c, place, part],
                near_send_sem.at[0],
                near_sem.at[0],
                2 * chip + c,
            ).start()
        return carry

    lax.fori_loop(1, KVH, near_out, 0)

    load_k.wait()
    load_v.wait()

    def picked(head):
        block = jnp.int32(0)
        count = vc[head]
        for t in range(DEV):
            entry = vb[head, t]
            mine = (lax.shift_right_logical(entry, 3) == me) & (t < count)
            block = block + jnp.where(mine, entry - OWN * me, 0)
        return block

    def pick(head, buffer, slot):
        block = picked(head)
        cols = columns(lax.div(head, H // KVH))
        buffer[slot, 0] = pkb[block, :, cols]
        buffer[slot, 1] = pvb[block, :, cols]

    def far_out(j, carry):
        head = lax.rem(me + j, DEV)
        pick(head, far_send, head)
        remote(far_send.at[head], far.at[me], far_send_sem, far_sem, head).start()
        return carry

    lax.fori_loop(1, DEV, far_out, 0)
    pick(me, far, me)

    own_k.wait()
    own_v.wait()
    first = OWN * (1 - odd)
    other = OWN * odd
    mine = kv.at[c, pl.ds(first, OWN)]
    wait_bytes(kv.at[c, pl.ds(first, OWN - 1)], near_sem.at[0])
    remote(mine, mine, near_send_sem.at[1], near_sem.at[1], sibling).start()
    remote(mine, mine, near_send_sem.at[2], near_sem.at[2], across).start()

    def q_out(j, carry):
        head = lax.rem(me - j + DEV, DEV)
        remote(q.at[:, columns(head)], qb.at[me], q_send_sem, q_sem.at[z], head).start()
        return carry

    lax.fori_loop(1, DEV, q_out, 0)

    count = vc[me]
    lane = lax.broadcasted_iota(jnp.int32, (1, FAR), 1)
    slot = lax.shift_right_logical(lane, 6)
    live = jnp.zeros((1, FAR), jnp.int32)
    for t in range(DEV):
        owner = jnp.where(t < count, lax.shift_right_logical(vb[me, t], 3), -1)
        live = jnp.where(slot == owner, 1, live)
    far_bias[...] = jnp.where(live > 0, 0.0, NEG)
    key = lax.broadcasted_iota(jnp.int32, (BLK, NEAR), 1)
    row = lax.broadcasted_iota(jnp.int32, (BLK, NEAR), 0)
    tri[...] = jnp.where((key < BLK) & (key > row), NEG, 0.0)

    theirs = kv.at[c, pl.ds(other, OWN)]
    wait_bytes(theirs, near_sem.at[2])
    remote(theirs, theirs, near_send_sem.at[3], near_sem.at[3], sibling).start()

    wait_bytes(far_send.at[pl.ds(0, DEV - 1)], far_sem)
    wait_bytes(mine, near_sem.at[1])
    wait_bytes(theirs, near_sem.at[3])

    near_slot = lax.shift_right_logical(lax.broadcasted_iota(jnp.int32, (1, NEAR), 1), 6)
    nt = (((1,), (1,)), ((), ()))
    nn = (((1,), (0,)), ((), ()))

    def step(t, carry):
        chip = lax.rem(z + t, CHIPS)
        wait_bytes(qb.at[pl.ds(2 * chip, 2)], q_sem.at[chip])
        rows = qb[pl.ds(2 * chip, 2)].reshape(2 * TOK, HD)
        far_keys = far[:, 0].reshape(FAR, HD)
        far_values = far[:, 1].reshape(FAR, HD)
        far_scores = lax.dot_general(rows, far_keys, nt, preferred_element_type=jnp.float32)
        far_scores = far_scores + far_bias[...]
        far_top = jnp.max(far_scores, 1, keepdims=True)
        tops, near_scores, near_values = [], [], []
        for b in range(4):
            block = 4 * chip + b
            keys, values = [], []
            bias = jnp.zeros((1, NEAR), jnp.float32)
            for s in range(SMAX):
                offset = so[me, s]
                target = jnp.maximum(block - offset, 0)
                their_chip = lax.shift_right_logical(target, 2)
                core = lax.shift_right_logical(target, 1) & 1
                place = (their_chip - 2 * g - 1) & (CHIPS - 1)
                half = target & 1
                keys.append(kv[core, place, 0, half])
                values.append(kv[core, place, 1, half])
                seen = (block >= offset) & (s < sc[me])
                bias = jnp.where(near_slot == s, jnp.where(seen, 0.0, NEG), bias)
            scores = lax.dot_general(
                rows[b * BLK : (b + 1) * BLK],
                jnp.concatenate(keys, 0),
                nt,
                preferred_element_type=jnp.float32,
            )
            scores = scores + (tri[...] + bias)
            near_scores.append(scores)
            near_values.append(jnp.concatenate(values, 0))
            tops.append(jnp.max(scores, 1, keepdims=True))
        top = jnp.maximum(far_top, jnp.concatenate(tops, 0)) * SCALE
        far_weights = jnp.exp2(far_scores * SCALE - top)
        total = jnp.sum(far_weights, 1, keepdims=True)
        mixed = lax.dot_general(
            far_weights.astype(jnp.bfloat16), far_values, nn, preferred_element_type=jnp.float32
        )
        for b in range(4):
            own = slice(b * BLK, (b + 1) * BLK)
            weights = jnp.exp2(near_scores[b] * SCALE - top[own])
            sums = total[own] + jnp.sum(weights, 1, keepdims=True)
            near_mixed = lax.dot_general(
                weights.astype(jnp.bfloat16),
                near_values[b],
                nn,
                preferred_element_type=jnp.float32,
            )
            done = (mixed[own] + near_mixed) / sums
            ob[2 * chip + b // 2, pl.ds((b % 2) * BLK, BLK), :] = done.astype(jnp.bfloat16)
        for core in range(2):
            device = 2 * chip + core

            @pl.when(device == me)
            def _():
                pltpu.make_async_copy(ob.at[device], out.at[:, columns(me)], out_sem).start()

            @pl.when(device != me)
            def _():
                remote(
                    ob.at[device], out.at[:, columns(me)], out_send_sem, out_sem, device
                ).start()

        return carry

    lax.fori_loop(0, CHIPS, step, 0)

    wait_bytes(ob, out_sem)
    most = ob.at[pl.ds(0, DEV - 1)]
    wait_bytes(most, out_send_sem)
    wait_bytes(most, q_send_sem)
    wait_bytes(far_send.at[pl.ds(0, DEV - 1)], far_send_sem)
    wait_bytes(kv.at[0, pl.ds(0, KVH - 1)], near_send_sem.at[0])
    wait_bytes(mine, near_send_sem.at[1])
    wait_bytes(mine, near_send_sem.at[2])
    wait_bytes(theirs, near_send_sem.at[3])


def shards(q, k, v, pk, pv, vb, vc, so, sc):
    hbm = pl.BlockSpec(memory_space=pl.ANY)
    smem = pl.BlockSpec(memory_space=pltpu.SMEM)
    dma = pltpu.SemaphoreType.DMA
    bf16 = jnp.bfloat16
    return pl.pallas_call(
        kernel,
        out_shape=jax.ShapeDtypeStruct((TOK, H * HD), bf16),
        in_specs=[hbm] * 5 + [smem] * 4,
        out_specs=hbm,
        scratch_shapes=[
            pltpu.VMEM((2, CHIPS, 2, 2, BLK, HD), bf16),
            pltpu.VMEM((DEV, 2, BLK, HD), bf16),
            pltpu.VMEM((DEV, 2, BLK, HD), bf16),
            pltpu.VMEM((OWN, BLK, KVH * HD), bf16),
            pltpu.VMEM((OWN, BLK, KVH * HD), bf16),
            pltpu.VMEM((DEV, TOK, HD), bf16),
            pltpu.VMEM((DEV, TOK, HD), bf16),
            pltpu.VMEM((1, FAR), jnp.float32),
            pltpu.VMEM((BLK, NEAR), jnp.float32),
            dma((4,)),
            dma((4,)),
            dma((4,)),
            dma,
            dma,
            dma((CHIPS,)),
            dma,
            dma,
            dma,
        ],
        compiler_params=pltpu.CompilerParams(
            collective_id=0, has_side_effects=True, vmem_limit_bytes=48 << 20
        ),
    )(
        q,
        k.reshape(2, BLK, KVH * HD),
        v.reshape(2, BLK, KVH * HD),
        pk.reshape(OWN, BLK, KVH * HD),
        pv.reshape(OWN, BLK, KVH * HD),
        vb,
        vc,
        so,
        sc,
    )


def solution(mesh):
    tokens = P(("req", "head"), None)
    return jax.shard_map(
        shards,
        mesh=mesh,
        in_specs=(tokens,) * 5 + (P("req", None), P("req"), P("req", None), P("req")),
        out_specs=tokens,
        check_vma=False,
    )
```

time: 508 us -> 193 us (0.38)
  waiting for transfers between devices: 229 us -> 0 us
  Pallas kernels: 0 us -> 185 us
  local copies, waits for them, and re-layouts: 79.3 us -> 7.9 us
  blocking collectives: 60.4 us -> 0 us
  matrix products: 51.3 us -> 0 us
  other arithmetic: 42 us -> 0 us
  starting transfers between devices: 37.1 us -> 0 us
  loops' own time: 5.78 us -> 0 us
    all_to_all x5 -> x0, waiting for transfers between devices: 229 us -> none  [the longest x1 55.8 us: shards(): lax.all_to_all(repeat_heads(keys_new), 'head', split_axis=1, concat_axis=...]
    pallas_call x0 -> x1, Pallas kernels: none -> 185 us  [shards(): pl.pallas_call(kernel, out_shape=jax.ShapeDtypeStruct((TOK, H * HD), bf16...]
    all_to_all x1 -> x0, blocking collectives: 60.4 us -> none  [shards(): lax.all_to_all(outputs, 'head', split_axis=0, concat_axis=1, tiled=True)]
    dot_general x32 -> x0, matrix products: 51.3 us -> none  [the longest x8 29.7 us: group_output(): jnp.einsum('rd,kd->rk', q_rows, flat_keys, preferred_element_type=jnp.flo...]
    all_to_all x5 -> x0, starting transfers between devices: 37.1 us -> none  [the longest x1 16.8 us: shards(): lax.all_to_all(send_keys, 'head', split_axis=0, concat_axis=0, tiled=True)]
    gather x18 -> x0, local copies, waits for them, and re-layouts: 34.5 us -> none  [the longest x8 15.8 us: slash_part(): near_keys = key_blocks[picked].reshape(row_blocks, -1, HD)]
    reduce_sum x16 -> x0, other arithmetic: 28.4 us -> none  [group_output(): row_total = jnp.sum(far_weights, 2) + jnp.sum(near_weights, 2)]
    dynamic_slice x20 -> x0, local copies, waits for them, and re-layouts: 18.2 us -> none  [the longest x8 10.1 us: attend(): return lax.map(group_output, starts).reshape(span_rows, HD)]
  transfers between devices with their start and end apart: 5 -> 0, of which waited for: 5 -> 0; matrix products, arithmetic and copies ran while one was open for 1% -> 0% of each run, Pallas kernels for 0% -> 0%
where the time goes in v1:
time: 193 us
  Pallas kernels  185 us (96%)
  local copies, waits for them, and re-layouts  7.9 us (4%)
    pallas_call x1, Pallas kernels, shards(): pl.pallas_call(kernel, out_shape=jax.ShapeDtypeStruct((TOK, H * HD), bf16...  185 us
    unnamed x20, local copies, waits for them, and re-layouts  7.9 us

profile of v1, /device:TPU:1, one launch (start us, length us, event | category | flops | bytes accessed | tf_op | source)
XLA Modules:
  0.0 192.6 jit_solution(7169992178317889645)
XLA Ops:
  0.0 0.0 copy-start.8
  0.0 0.0 copy-start.5
  0.0 0.7 copy-done.8
  0.7 0.0 copy-start.6
  0.7 0.0 copy-start.7
  0.7 0.1 copy.10.so
  0.8 0.0 copy-done.5
  0.8 0.6 copy-done.6
  1.3 0.0 copy-done.7
  1.4 0.0 copy-start
  1.4 1.2 copy-done
  2.6 0.0 copy-start.1
  2.6 1.2 copy-done.1
  3.8 0.0 copy-start.2
  3.8 1.2 copy-done.2
  5.0 0.0 copy-start.3
  5.0 0.9 copy-done.3
  6.0 0.0 copy-start.4
  6.0 0.9 copy-done.4
  6.9 184.7 %shard_map.91 = bf16[128,4096]{1,0:T(8,128)(2,1)S(1)} custom-call(bf16[128,4096]{1,0:T(8,128)(2,1)S(1)} %copy-done, bf16[2,64,1024]{2,1,0:T(8,128)(2,1)S(1)} %bitcast.6, bf16[2,64,1024]{2,1,0:T(8,128)(2,1)S(1)} %bitcast.7, bf16[8,64,1024]{2,1,0:T(8,128)(2,1)S(1)} %bitcast.4, bf16[8,64,1024]{2,1,0:T(8,128)(2,1)S(1)} %bitcast.5, s32[32,32]{1,0:T(8,128)S(1)} %copy-done.5, ...), custom_call_target="tpu_custom_call" | custom-call | tf_op jit(solution)/shard_map/pallas_call | solution.py:270
  191.7 1.0 copy.12
Async XLA Ops:
  0.0 0.7 copy-start.8
  0.0 0.8 copy-start.5
  0.7 0.7 copy-start.6
  0.7 0.7 copy-start.7
  1.4 1.2 copy-start
  2.6 1.2 copy-start.1
  3.8 1.2 copy-start.2
  5.0 0.9 copy-start.3
  6.0 0.9 copy-start.4

commit v2 on v1

--- a/solution.py
+++ b/solution.py
@@ -29,10 +29,10 @@
     v,
     pk,
     pv,
-    vb,
-    vc,
-    so,
-    sc,
+    vb_hbm,
+    vc_hbm,
+    so_hbm,
+    sc_hbm,
     out,
     kv,
     far,
@@ -43,6 +43,10 @@
     ob,
     far_bias,
     tri,
+    vb,
+    vc,
+    so,
+    sc,
     load_sem,
     near_sem,
     near_send_sem,
@@ -75,15 +79,35 @@
     def wait_bytes(ref, sem):
         pltpu.make_async_copy(ref, ref, sem).wait()
 
+    def turn(t):
+        return jnp.where(lax.rem(t, 2) == 1, 8 - lax.div(t + 1, 2), lax.div(t, 2) - 8)
+
+    def signal(semaphore, device):
+        pl.semaphore_signal(semaphore, inc=1, device_id={"head": device}, device_id_type=MESH)
+
+    right = lax.rem(z + 1, CHIPS)
+    left = lax.rem(z + CHIPS - 1, CHIPS)
     barrier = pltpu.get_barrier_semaphore()
 
-    def greet(j, carry):
-        pl.semaphore_signal(
-            barrier, inc=1, device_id={"head": lax.rem(me + j, DEV)}, device_id_type=MESH
+    def greet(t, carry):
+        chip = lax.rem(z + turn(t) + CHIPS, CHIPS)
+        for core in range(2):
+
+            @pl.when(2 * chip + core != me)
+            def _():
+                signal(barrier, 2 * chip + core)
+
+        return carry
+
+    lax.fori_loop(0, CHIPS, greet, 0)
+    metas = [
+        pltpu.make_async_copy(source, target, load_sem.at[4 + i])
+        for i, (source, target) in enumerate(
+            ((vb_hbm, vb), (vc_hbm, vc), (so_hbm, so), (sc_hbm, sc))
         )
-        return carry
-
-    lax.fori_loop(1, DEV, greet, 0)
+    ]
+    for copy in metas:
+        copy.start()
     load_k = pltpu.make_async_copy(pk, pkb, load_sem.at[0])
     load_v = pltpu.make_async_copy(pv, pvb, load_sem.at[1])
     load_k.start()
@@ -96,11 +120,8 @@
     own_v.start()
     pltpu.make_async_copy(q.at[:, columns(me)], qb.at[me], q_sem.at[z]).start()
 
-    pl.semaphore_wait(barrier, DEV - 1)
-
-    def near_out(j, carry):
-        group = lax.rem(g + j, KVH)
-        chip = 2 * group + lax.div(lax.rem(2 * group - z + CHIPS, CHIPS), CHIPS // 2)
+    def near_out(chip):
+        group = lax.div(chip, 2)
         place = lax.rem(z - 2 * group - 1 + 2 * CHIPS, CHIPS)
         for part, source in enumerate((k, v)):
             remote(
@@ -110,12 +131,6 @@
                 near_sem.at[0],
                 2 * chip + c,
             ).start()
-        return carry
-
-    lax.fori_loop(1, KVH, near_out, 0)
-
-    load_k.wait()
-    load_v.wait()
 
     def picked(head):
         block = jnp.int32(0)
@@ -132,13 +147,43 @@
         buffer[slot, 0] = pkb[block, :, cols]
         buffer[slot, 1] = pvb[block, :, cols]
 
-    def far_out(j, carry):
-        head = lax.rem(me + j, DEV)
+    def far_out(head):
         pick(head, far_send, head)
         remote(far_send.at[head], far.at[me], far_send_sem, far_sem, head).start()
-        return carry
-
-    lax.fori_loop(1, DEV, far_out, 0)
+
+    for copy in metas:
+        copy.wait()
+    load_k.wait()
+    load_v.wait()
+    pl.semaphore_wait(barrier, DEV - 1)
+
+    def near_step(j, carry):
+        ahead = lax.rem(z + j, CHIPS)
+        behind = lax.rem(z - j + CHIPS, CHIPS)
+
+        @pl.when(lax.rem(ahead, 2) == 0)
+        def _():
+            near_out(ahead)
+
+        @pl.when(lax.rem(behind, 2) == 1)
+        def _():
+            near_out(behind)
+
+        return carry
+
+    lax.fori_loop(1, KVH, near_step, 0)
+
+    def far_step(t, carry):
+        chip = lax.rem(z + turn(t) + CHIPS, CHIPS)
+        for core in range(2):
+
+            @pl.when(2 * chip + core != me)
+            def _():
+                far_out(2 * chip + core)
+
+        return carry
+
+    lax.fori_loop(0, CHIPS, far_step, 0)
     pick(me, far, me)
 
     own_k.wait()
@@ -150,12 +195,20 @@
     remote(mine, mine, near_send_sem.at[1], near_sem.at[1], sibling).start()
     remote(mine, mine, near_send_sem.at[2], near_sem.at[2], across).start()
 
-    def q_out(j, carry):
-        head = lax.rem(me - j + DEV, DEV)
-        remote(q.at[:, columns(head)], qb.at[me], q_send_sem, q_sem.at[z], head).start()
-        return carry
-
-    lax.fori_loop(1, DEV, q_out, 0)
+    def q_out(t, carry):
+        chip = lax.rem(z - turn(t) + CHIPS, CHIPS)
+        for core in range(2):
+            device = 2 * chip + core
+
+            @pl.when(device != me)
+            def _():
+                remote(
+                    q.at[:, columns(device)], qb.at[me], q_send_sem, q_sem.at[z], device
+                ).start()
+
+        return carry
+
+    lax.fori_loop(0, 16, q_out, 0)
 
     count = vc[me]
     lane = lax.broadcasted_iota(jnp.int32, (1, FAR), 1)
@@ -182,7 +235,7 @@
     nn = (((1,), (0,)), ((), ()))
 
     def step(t, carry):
-        chip = lax.rem(z + t, CHIPS)
+        chip = lax.rem(z + turn(t) + CHIPS, CHIPS)
         wait_bytes(qb.at[pl.ds(2 * chip, 2)], q_sem.at[chip])
         rows = qb[pl.ds(2 * chip, 2)].reshape(2 * TOK, HD)
         far_keys = far[:, 0].reshape(FAR, HD)
@@ -196,7 +249,7 @@
             keys, values = [], []
             bias = jnp.zeros((1, NEAR), jnp.float32)
             for s in range(SMAX):
-                offset = so[me, s]
+                offset = so[s, me]
                 target = jnp.maximum(block - offset, 0)
                 their_chip = lax.shift_right_logical(target, 2)
                 core = lax.shift_right_logical(target, 1) & 1
@@ -264,13 +317,12 @@
 
 def shards(q, k, v, pk, pv, vb, vc, so, sc):
     hbm = pl.BlockSpec(memory_space=pl.ANY)
-    smem = pl.BlockSpec(memory_space=pltpu.SMEM)
     dma = pltpu.SemaphoreType.DMA
     bf16 = jnp.bfloat16
     return pl.pallas_call(
         kernel,
         out_shape=jax.ShapeDtypeStruct((TOK, H * HD), bf16),
-        in_specs=[hbm] * 5 + [smem] * 4,
+        in_specs=[hbm] * 9,
         out_specs=hbm,
         scratch_shapes=[
             pltpu.VMEM((2, CHIPS, 2, 2, BLK, HD), bf16),
@@ -282,9 +334,13 @@
             pltpu.VMEM((DEV, TOK, HD), bf16),
             pltpu.VMEM((1, FAR), jnp.float32),
             pltpu.VMEM((BLK, NEAR), jnp.float32),
+            pltpu.SMEM((DEV, DEV), jnp.int32),
+            pltpu.SMEM((DEV,), jnp.int32),
+            pltpu.SMEM((SMAX, DEV), jnp.int32),
+            pltpu.SMEM((DEV,), jnp.int32),
+            dma((8,)),
             dma((4,)),
             dma((4,)),
-            dma((4,)),
             dma,
             dma,
             dma((CHIPS,)),
@@ -293,7 +349,7 @@
             dma,
         ],
         compiler_params=pltpu.CompilerParams(
-            collective_id=0, has_side_effects=True, vmem_limit_bytes=48 << 20
+            collective_id=0, has_side_effects=True, vmem_limit_bytes=60 << 20
         ),
     )(
         q,
@@ -303,7 +359,7 @@
         pv.reshape(OWN, BLK, KVH * HD),
         vb,
         vc,
-        so,
+        so.T,
         sc,
     )
 

time: 193 us -> 184 us (0.953)
  local copies, waits for them, and re-layouts: 7.9 us -> 2.29 us
  Pallas kernels: 185 us -> 182 us
    unnamed x20 -> x1, local copies, waits for them, and re-layouts: 7.9 us -> 2.29 us
    pallas_call x1, Pallas kernels: 185 us -> 182 us  [shards(): pl.pallas_call(kernel, out_shape=jax.ShapeDtypeStruct((TOK, H * HD), bf16...]
where the time goes in v2:
time: 184 us
  Pallas kernels  182 us (99%)
  local copies, waits for them, and re-layouts  2.29 us (1%)
    pallas_call x1, Pallas kernels, shards(): pl.pallas_call(kernel, out_shape=jax.ShapeDtypeStruct((TOK, H * HD), bf16...  182 us

profile of v2, /device:TPU:1, one launch (start us, length us, event | category | flops | bytes accessed | tf_op | source)
XLA Modules:
  0.0 184.1 jit_solution(17806915274265113259)
XLA Ops:
  0.0 181.8 %shard_map.91 = bf16[128,4096]{1,0:T(8,128)(2,1)} custom-call(bf16[128,4096]{1,0:T(8,128)(2,1)} %q.1, bf16[2,64,1024]{2,1,0:T(8,128)(2,1)} %bitcast.7, bf16[2,64,1024]{2,1,0:T(8,128)(2,1)} %bitcast.8, bf16[8,64,1024]{2,1,0:T(8,128)(2,1)} %bitcast.5, bf16[8,64,1024]{2,1,0:T(8,128)(2,1)} %bitcast.6, s32[32,32]{1,0:T(8,128)} %vb_hbm.1, s32[32]{0:T(128)} %vc_hbm.1, ...), custom_call_target="tpu_custom_call" | custom-call | tf_op jit(solution)/shard_map/pallas_call | solution.py:322
  181.8 2.3 %copy.11 = bf16[128,4096]{1,0:T(8,128)(2,1)} copy(bf16[128,4096]{1,0:T(8,128)(2,1)} %shard_map.91) | data formatting | bytes 2097152

commit v3 on v2

--- a/solution.py
+++ b/solution.py
@@ -18,6 +18,7 @@
 TOK = 128
 FAR = DEV * BLK
 NEAR = SMAX * BLK
+RADIUS = 2
 MESH = pl.DeviceIdType.MESH
 SCALE = math.log2(math.e) / math.sqrt(HD)
 NEG = -math.inf
@@ -56,6 +57,7 @@
     q_send_sem,
     out_sem,
     out_send_sem,
+    known_sem,
 ):
     me = lax.axis_index("head")
     z, c = lax.div(me, 2), lax.rem(me, 2)
@@ -85,21 +87,12 @@
     def signal(semaphore, device):
         pl.semaphore_signal(semaphore, inc=1, device_id={"head": device}, device_id_type=MESH)
 
-    right = lax.rem(z + 1, CHIPS)
-    left = lax.rem(z + CHIPS - 1, CHIPS)
     barrier = pltpu.get_barrier_semaphore()
-
-    def greet(t, carry):
-        chip = lax.rem(z + turn(t) + CHIPS, CHIPS)
-        for core in range(2):
-
-            @pl.when(2 * chip + core != me)
-            def _():
+    signal(barrier, sibling)
+    for distance in range(1, RADIUS + 1):
+        for chip in (lax.rem(z + distance, CHIPS), lax.rem(z + CHIPS - distance, CHIPS)):
+            for core in range(2):
                 signal(barrier, 2 * chip + core)
-
-        return carry
-
-    lax.fori_loop(0, CHIPS, greet, 0)
     metas = [
         pltpu.make_async_copy(source, target, load_sem.at[4 + i])
         for i, (source, target) in enumerate(
@@ -155,11 +148,11 @@
         copy.wait()
     load_k.wait()
     load_v.wait()
-    pl.semaphore_wait(barrier, DEV - 1)
-
-    def near_step(j, carry):
-        ahead = lax.rem(z + j, CHIPS)
-        behind = lax.rem(z - j + CHIPS, CHIPS)
+    pl.semaphore_wait(barrier, 4 * RADIUS + 1)
+
+    def serve(distance, carry):
+        ahead = lax.rem(z + distance, CHIPS)
+        behind = lax.rem(z + CHIPS - distance, CHIPS)
 
         @pl.when(lax.rem(ahead, 2) == 0)
         def _():
@@ -171,7 +164,14 @@
 
         return carry
 
-    lax.fori_loop(1, KVH, near_step, 0)
+    done, reach, rounds = 0, RADIUS, 0
+    while reach < CHIPS // 2:
+        for chip in (lax.rem(z + reach, CHIPS), lax.rem(z + CHIPS - reach, CHIPS)):
+            signal(known_sem.at[rounds], 2 * chip + c)
+        lax.fori_loop(done + 1, reach + 1, serve, 0)
+        pl.semaphore_wait(known_sem.at[rounds], 2)
+        done, reach, rounds = reach, 2 * reach, rounds + 1
+    lax.fori_loop(done + 1, CHIPS // 2, serve, 0)
 
     def far_step(t, carry):
         chip = lax.rem(z + turn(t) + CHIPS, CHIPS)
@@ -347,6 +347,7 @@
             dma,
             dma,
             dma,
+            pltpu.SemaphoreType.REGULAR((4,)),
         ],
         compiler_params=pltpu.CompilerParams(
             collective_id=0, has_side_effects=True, vmem_limit_bytes=60 << 20

time: 184 us -> 181 us (0.984)
  Pallas kernels: 182 us -> 179 us
    pallas_call x1, Pallas kernels: 182 us -> 179 us  [shards(): pl.pallas_call(kernel, out_shape=jax.ShapeDtypeStruct((TOK, H * HD), bf16...]
where the time goes in v3:
time: 181 us
  Pallas kernels  179 us (99%)
  local copies, waits for them, and re-layouts  2.29 us (1%)
    pallas_call x1, Pallas kernels, shards(): pl.pallas_call(kernel, out_shape=jax.ShapeDtypeStruct((TOK, H * HD), bf16...  179 us

profile of v3, /device:TPU:1, one launch (start us, length us, event | category | flops | bytes accessed | tf_op | source)
XLA Modules:
  0.0 181.1 jit_solution(1539069237887535334)
XLA Ops:
  0.0 178.8 %shard_map.91 = bf16[128,4096]{1,0:T(8,128)(2,1)} custom-call(bf16[128,4096]{1,0:T(8,128)(2,1)} %q.1, bf16[2,64,1024]{2,1,0:T(8,128)(2,1)} %bitcast.7, bf16[2,64,1024]{2,1,0:T(8,128)(2,1)} %bitcast.8, bf16[8,64,1024]{2,1,0:T(8,128)(2,1)} %bitcast.5, bf16[8,64,1024]{2,1,0:T(8,128)(2,1)} %bitcast.6, s32[32,32]{1,0:T(8,128)} %vb_hbm.1, s32[32]{0:T(128)} %vc_hbm.1, ...), custom_call_target="tpu_custom_call" | custom-call | tf_op jit(solution)/shard_map/pallas_call | solution.py:322
  178.8 2.3 %copy.11 = bf16[128,4096]{1,0:T(8,128)(2,1)} copy(bf16[128,4096]{1,0:T(8,128)(2,1)} %shard_map.91) | data formatting | bytes 2097152

commit v4 on v3

--- a/solution.py
+++ b/solution.py
@@ -84,6 +84,12 @@
     def turn(t):
         return jnp.where(lax.rem(t, 2) == 1, 8 - lax.div(t + 1, 2), lax.div(t, 2) - 8)
 
+    def mixed(t):
+        pair = lax.div(t + 1, 2)
+        distance = jnp.where(lax.rem(pair, 2) == 1, 8 - lax.div(pair + 1, 2), lax.div(pair, 2))
+        distance = jnp.where(t == 0, 8, jnp.where(t == 15, 0, distance))
+        return jnp.where(lax.rem(t, 2) == 1, distance, -distance)
+
     def signal(semaphore, device):
         pl.semaphore_signal(semaphore, inc=1, device_id={"head": device}, device_id_type=MESH)
 
@@ -174,7 +180,7 @@
     lax.fori_loop(done + 1, CHIPS // 2, serve, 0)
 
     def far_step(t, carry):
-        chip = lax.rem(z + turn(t) + CHIPS, CHIPS)
+        chip = lax.rem(z + mixed(t) + CHIPS, CHIPS)
         for core in range(2):
 
             @pl.when(2 * chip + core != me)
@@ -196,7 +202,7 @@
     remote(mine, mine, near_send_sem.at[2], near_sem.at[2], across).start()
 
     def q_out(t, carry):
-        chip = lax.rem(z - turn(t) + CHIPS, CHIPS)
+        chip = lax.rem(z - mixed(t) + CHIPS, CHIPS)
         for core in range(2):
             device = 2 * chip + core
 
@@ -321,9 +327,9 @@
     bf16 = jnp.bfloat16
     return pl.pallas_call(
         kernel,
-        out_shape=jax.ShapeDtypeStruct((TOK, H * HD), bf16),
+        out_shape=pltpu.VMEM((TOK, H * HD), bf16),
         in_specs=[hbm] * 9,
-        out_specs=hbm,
+        out_specs=pl.BlockSpec(memory_space=pltpu.VMEM),
         scratch_shapes=[
             pltpu.VMEM((2, CHIPS, 2, 2, BLK, HD), bf16),
             pltpu.VMEM((DEV, 2, BLK, HD), bf16),

time: 181 us -> 180 us (level)
  no operation moved by 1% of the time
where the time goes in v4:
time: 180 us; the launch traced here: 179 us
  Pallas kernels  178 us (99%)
    pallas_call x1, Pallas kernels, shards(): pl.pallas_call(kernel, out_shape=pltpu.VMEM((TOK, H * HD), bf16), in_spec...  178 us

profile of v4, /device:TPU:1, one launch (start us, length us, event | category | flops | bytes accessed | tf_op | source)
XLA Modules:
  0.0 179.4 jit_solution(1648738388266102383)
XLA Ops:
  0.0 178.4 %shard_map.91 = bf16[128,4096]{1,0:T(8,128)(2,1)S(1)} custom-call(bf16[128,4096]{1,0:T(8,128)(2,1)} %q.1, bf16[2,64,1024]{2,1,0:T(8,128)(2,1)} %bitcast.7, bf16[2,64,1024]{2,1,0:T(8,128)(2,1)} %bitcast.8, bf16[8,64,1024]{2,1,0:T(8,128)(2,1)} %bitcast.5, bf16[8,64,1024]{2,1,0:T(8,128)(2,1)} %bitcast.6, s32[32,32]{1,0:T(8,128)} %vb_hbm.1, s32[32]{0:T(128)} %vc_hbm.1, ...), custom_call_target="tpu_custom_call" | custom-call | tf_op jit(solution)/shard_map/pallas_call | solution.py:328
  178.4 1.0 copy.11

commit v5 on v4

--- a/solution.py
+++ b/solution.py
@@ -150,10 +150,6 @@
         pick(head, far_send, head)
         remote(far_send.at[head], far.at[me], far_send_sem, far_sem, head).start()
 
-    for copy in metas:
-        copy.wait()
-    load_k.wait()
-    load_v.wait()
     pl.semaphore_wait(barrier, 4 * RADIUS + 1)
 
     def serve(distance, carry):
@@ -177,7 +173,12 @@
         lax.fori_loop(done + 1, reach + 1, serve, 0)
         pl.semaphore_wait(known_sem.at[rounds], 2)
         done, reach, rounds = reach, 2 * reach, rounds + 1
-    lax.fori_loop(done + 1, CHIPS // 2, serve, 0)
+    for distance in range(CHIPS // 2 - 1, done, -1):
+        serve(distance, 0)
+    for copy in metas:
+        copy.wait()
+    load_k.wait()
+    load_v.wait()
 
     def far_step(t, carry):
         chip = lax.rem(z + mixed(t) + CHIPS, CHIPS)
@@ -198,8 +199,8 @@
     other = OWN * odd
     mine = kv.at[c, pl.ds(first, OWN)]
     wait_bytes(kv.at[c, pl.ds(first, OWN - 1)], near_sem.at[0])
+    remote(mine, mine, near_send_sem.at[2], near_sem.at[2], across).start()
     remote(mine, mine, near_send_sem.at[1], near_sem.at[1], sibling).start()
-    remote(mine, mine, near_send_sem.at[2], near_sem.at[2], across).start()
 
     def q_out(t, carry):
         chip = lax.rem(z - mixed(t) + CHIPS, CHIPS)

time: 180 us -> 179 us (level)
  no operation moved by 1% of the time
where the time goes in v5:
time: 179 us
  Pallas kernels  178 us (99%)
    pallas_call x1, Pallas kernels, shards(): pl.pallas_call(kernel, out_shape=pltpu.VMEM((TOK, H * HD), bf16), in_spec...  178 us

profile of v5, /device:TPU:1, one launch (start us, length us, event | category | flops | bytes accessed | tf_op | source)
XLA Modules:
  0.0 179.1 jit_solution(16623005998705422895)
XLA Ops:
  0.0 178.2 %shard_map.91 = bf16[128,4096]{1,0:T(8,128)(2,1)S(1)} custom-call(bf16[128,4096]{1,0:T(8,128)(2,1)} %q.1, bf16[2,64,1024]{2,1,0:T(8,128)(2,1)} %bitcast.7, bf16[2,64,1024]{2,1,0:T(8,128)(2,1)} %bitcast.8, bf16[8,64,1024]{2,1,0:T(8,128)(2,1)} %bitcast.5, bf16[8,64,1024]{2,1,0:T(8,128)(2,1)} %bitcast.6, s32[32,32]{1,0:T(8,128)} %vb_hbm.1, s32[32]{0:T(128)} %vc_hbm.1, ...), custom_call_target="tpu_custom_call" | custom-call | tf_op jit(solution)/shard_map/pallas_call | solution.py:329
  178.2 1.0 copy.11
